TPU v7x, 32 devices: a whole 2x2x4 slice. The times are simulated.
32 devices in a mesh: dp: 4 (over x, core), ctx: 8 (over z, y).
Axes of the slice: x: 2, y: 2, z: 4, core: 2. Of those that a mesh axis runs over, the one named last changes fastest.
Arguments:
- tokens: bfloat16 [8, 1024, 2048], P('dp', 'ctx'), may hold values from -6 to 6
- cotangent: bfloat16 [8, 1024, 2048], P('dp', 'ctx'), may hold values from -6 to 6
- block_order: int32 [16], replicated, may hold values from 0 to 15, as said below
- attention_in: float32 [2048, 3072], P(('dp', 'ctx')), may hold values from -0.125 to 0.125
- attention_out: float32 [2048, 2048], P(('dp', 'ctx')), may hold values from -0.75 to 0.75
- gate_up: float32 [2048, 16384], P(('dp', 'ctx')), may hold values from -0.125 to 0.125
- down_matrix: float32 [8192, 2048], P(('dp', 'ctx')), may hold values from -0.0625 to 0.0625
- gains: float32 [2, 2048], P(None, ('dp', 'ctx')), may hold values from 0.5 to 1.5
- mean_attention_in: float32 [2048, 3072], P(('dp', 'ctx')), may hold values from -32 to 32
- mean_attention_out: float32 [2048, 2048], P(('dp', 'ctx')), may hold values from -12 to 12
- mean_gate_up: float32 [2048, 16384], P(('dp', 'ctx')), may hold values from -16 to 16
- mean_down: float32 [8192, 2048], P(('dp', 'ctx')), may hold values from -32 to 32
- mean_gains: float32 [2, 2048], P(None, ('dp', 'ctx')), may hold values from -64 to 64
- square_attention_in: float32 [2048, 3072], P(('dp', 'ctx')), may hold values from 108.1344 to 430.8992
- square_attention_out: float32 [2048, 2048], P(('dp', 'ctx')), may hold values from 17.2032 to 68.8128
- square_gate_up: float32 [2048, 16384], P(('dp', 'ctx')), may hold values from 38.5024 to 155.648
- square_down: float32 [8192, 2048], P(('dp', 'ctx')), may hold values from 155.648 to 622.592
- square_gains: float32 [2, 2048], P(None, ('dp', 'ctx')), may hold values from 430.8992 to 1720.32
Outputs:
- block_out: bfloat16 [8, 1024, 2048], P('dp', 'ctx')
- tokens_grad: float32 [8, 1024, 2048], P('dp', 'ctx')
- new_mean_attention_in: float32 [2048, 3072], P(('dp', 'ctx'))
- new_square_attention_in: float32 [2048, 3072], P(('dp', 'ctx'))
- new_attention_in: float32 [2048, 3072], P(('dp', 'ctx'))
- new_mean_attention_out: float32 [2048, 2048], P(('dp', 'ctx'))
- new_square_attention_out: float32 [2048, 2048], P(('dp', 'ctx'))
- new_attention_out: float32 [2048, 2048], P(('dp', 'ctx'))
- new_mean_gate_up: float32 [2048, 16384], P(('dp', 'ctx'))
- new_square_gate_up: float32 [2048, 16384], P(('dp', 'ctx'))
- new_gate_up: float32 [2048, 16384], P(('dp', 'ctx'))
- new_mean_down: float32 [8192, 2048], P(('dp', 'ctx'))
- new_square_down: float32 [8192, 2048], P(('dp', 'ctx'))
- new_down_matrix: float32 [8192, 2048], P(('dp', 'ctx'))
- new_mean_gains: float32 [2, 2048], P(None, ('dp', 'ctx'))
- new_square_gains: float32 [2, 2048], P(None, ('dp', 'ctx'))
- new_gains: float32 [2, 2048], P(None, ('dp', 'ctx'))
Inputs may be any that keep to these rules, and one draw needn't show every extreme that they name: `block_order`: a permutation; the two entries 2c and 2c+1 of each device c sum to 15.
All inputs are finite; a program needn't handle non-finite values.
Results may differ from a plain program's by a relative error of at most 0.024.
Values may be sent and summed in bfloat16 or wider, within the bound.
A program may use at most 512 MiB of HBM per device.

v0:
```python
import functools

import jax
import jax.numpy as jnp
import numpy as np
from jax import lax
from jax.experimental import pallas as pl
from jax.experimental.pallas import tpu as pltpu
from jax.sharding import PartitionSpec as P

D = 2048
HEADS = 32
KV_HEADS = 8
HEAD = 64
FF = 8192
STEP = 5


norm_eps = 1e-05
rope_base = 500000.0
beta_one = 0.9
beta_two = 0.95
gain_rate = 1.25
input_boost = 2.5
weight_decay = 0.1
adam_eps = 1e-08
masked_score = -1e30


def norm_parts(values):
    factor = lax.rsqrt(jnp.mean(values * values, -1, keepdims=True) + norm_eps)
    return (values * factor, factor)


def norm_back(back_normed, normed, factor):
    return factor * (back_normed - normed * jnp.mean(back_normed * normed, -1, keepdims=True))


def adam_update(weight, gradient, first_moment, second_moment, step_rate, decay_rate):
    first_new = beta_one * first_moment + (1.0 - beta_one) * gradient
    second_new = beta_two * second_moment + (1.0 - beta_two) * gradient * gradient
    update = (
        first_new
        / (1.0 - beta_one**STEP)
        / (jnp.sqrt(second_new / (1.0 - beta_two**STEP)) + adam_eps)
    )
    return (first_new, second_new, weight - step_rate * (update + decay_rate * weight))


def line_groups(shards):
    return [[2 * s + half for s in range(shards // 2)] for half in (0, 1)]


def gather_line(rows):
    return lax.all_gather(
        rows, "ctx", axis=0, tiled=True, axis_index_groups=line_groups(lax.axis_size("ctx"))
    )


def sum_line(gradient):
    return lax.psum_scatter(
        gradient,
        "ctx",
        scatter_dimension=0,
        tiled=True,
        axis_index_groups=line_groups(lax.axis_size("ctx")),
    )


def dot_nn(a, b):
    return lax.dot_general(a, b, (((1,), (0,)), ((), ())), preferred_element_type=jnp.float32)


def dot_nt(a, b):
    return lax.dot_general(a, b, (((1,), (1,)), ((), ())), preferred_element_type=jnp.float32)


def dot_tn(a, b):
    return lax.dot_general(a, b, (((0,), (0,)), ((), ())), preferred_element_type=jnp.float32)


def causal_keep(tile):
    keys = lax.broadcasted_iota(jnp.int32, (tile, tile), 0)
    queries = lax.broadcasted_iota(jnp.int32, (tile, tile), 1)
    return keys <= queries


def turn_group(values, cos, sin, forward):
    lanes = lax.broadcasted_iota(jnp.int32, values.shape, 1)
    other = jnp.where(
        lanes % HEAD < HEAD // 2,
        pltpu.roll(values, 2 * HEAD - HEAD // 2, 1),
        pltpu.roll(values, HEAD // 2, 1),
    )
    if forward:
        return values * cos + other * sin
    return values * cos - other * sin


def turn_columns(values, start, turned_cols, cos, sin, forward):
    if start >= turned_cols:
        return values
    turned = turn_group(values, cos, sin, forward)
    if start + 2 * HEAD <= turned_cols:
        return turned
    lanes = lax.broadcasted_iota(jnp.int32, values.shape, 1)
    return jnp.where(lanes < turned_cols - start, turned, values)


def attend_kernel(
    q_heads,
    kv_heads,
    tile,
    order_ref,
    where_ref,
    all_qkv_ref,
    cos_ref,
    sin_ref,
    all_out_ref,
    all_lse_ref,
    all_kept_ref,
    made,
):
    for sequence in range(all_qkv_ref.shape[0]):
        attend_sequence(
            q_heads,
            kv_heads,
            tile,
            order_ref,
            where_ref,
            all_qkv_ref.at[sequence],
            cos_ref,
            sin_ref,
            all_out_ref.at[sequence],
            all_lse_ref.at[sequence],
            all_kept_ref.at[sequence],
            made,
        )


def attend_sequence(
    q_heads,
    kv_heads,
    tile,
    order_ref,
    where_ref,
    qkv_ref,
    cos_ref,
    sin_ref,
    out_ref,
    lse_ref,
    kept_ref,
    made,
):
    blocks, rows, cols = qkv_ref.shape
    length = blocks * rows
    group = q_heads // kv_heads
    q_cols, k_cols = q_heads * HEAD, kv_heads * HEAD
    scale = HEAD ** (-0.5)

    def take_block(i, _):
        start = pl.multiple_of(i * rows, rows)
        cos = cos_ref[i]
        sin = sin_ref[i]
        for c in range(0, cols, 2 * HEAD):
            values = qkv_ref[where_ref[i], :, c : c + 2 * HEAD]
            values = turn_columns(values, c, q_cols + k_cols, cos, sin, True)
            kept_ref[pl.ds(start, rows), c : c + 2 * HEAD] = values.astype(jnp.bfloat16)
        return 0

    lax.fori_loop(0, blocks, take_block, 0)
    keep = causal_keep(tile)
    for kv in range(kv_heads):
        k_at = q_cols + kv * HEAD
        v_at = q_cols + k_cols + kv * HEAD

        def query_step(i, _):
            q_start = pl.multiple_of(i * tile, tile)
            queries = [
                kept_ref[
                    pl.ds(q_start, tile), (kv * group + g) * HEAD : (kv * group + g + 1) * HEAD
                ]
                for g in range(group)
            ]

            def key_tile(j, carry, masked):
                k_start = pl.multiple_of(j * tile, tile)
                keys = kept_ref[pl.ds(k_start, tile), k_at : k_at + HEAD]
                values = kept_ref[pl.ds(k_start, tile), v_at : v_at + HEAD]
                result = []
                for g in range(group):
                    peak, total, weighted = carry[g]
                    scores = dot_nt(keys, queries[g]) * scale
                    if masked:
                        scores = jnp.where(keep, scores, masked_score)
                    new_peak = jnp.maximum(peak, jnp.max(scores, 0, keepdims=True))
                    weights = jnp.exp(scores - new_peak)
                    shrink = jnp.exp(peak - new_peak)
                    total = total * shrink + jnp.sum(weights, 0, keepdims=True)
                    weighted = weighted * shrink + dot_tn(values, weights.astype(jnp.bfloat16))
                    result.append((new_peak, total, weighted))
                return tuple(result)

            start = tuple(
                (
                    jnp.full((1, tile), masked_score, jnp.float32),
                    jnp.zeros((1, tile), jnp.float32),
                    jnp.zeros((HEAD, tile), jnp.float32),
                )
                for _ in range(group)
            )
            carry = lax.fori_loop(0, i, lambda j, c: key_tile(j, c, False), start)
            carry = key_tile(i, carry, True)
            for g in range(group):
                head = kv * group + g
                peak, total, weighted = carry[g]
                lse_ref[head : head + 1, pl.ds(q_start, tile)] = peak + jnp.log(total)
                made[pl.ds(i * (tile // rows), tile // rows), :, head * HEAD : (head + 1) * HEAD] = (
                    (weighted / total).T.astype(jnp.bfloat16).reshape(-1, rows, HEAD)
                )
            return 0

        lax.fori_loop(0, length // tile, query_step, 0)

    def give_block(i, _):
        out_ref[i] = made[order_ref[i]]
        return 0

    lax.fori_loop(0, blocks, give_block, 0)


def attend_back_kernel(
    q_heads,
    kv_heads,
    tile,
    steps,
    order_ref,
    where_ref,
    all_kept_ref,
    all_back_ref,
    all_lse_ref,
    cos_ref,
    sin_ref,
    out_rows,
    residual,
    out_parts,
    all_out_ref,
    block_out,
    out_sum,
    *scratch,
):
    me = (lax.axis_index("dp"), lax.axis_index("ctx"))
    slow = out_parts.shape[0]
    line = [(me[0], me[1] ^ (2 * by)) for by in range(1, slow)]
    greet(me, [member(me, by) for by in (1, 2, 4)] + line, [])
    work, line_out, scratch = scratch[:4], scratch[4:8], scratch[8:]
    scatter = GroupScatter(me, out_rows, scratch[:7], scratch[7:], steps)
    out_line = LineSum(me, slow, out_parts, line_out[:2], line_out[2:])

    def one():
        for k in range(steps):
            scatter.send_first(k)

    def two():
        for k in range(steps):
            scatter.send_second(k)

    def three():
        for k in range(steps):
            span = scatter.window(k)
            for part in (0, 1):
                value = residual[part, span] + scatter.total(k, part)
                block_out[part, span] = value.astype(jnp.bfloat16)

    tasks = [one, two, three]

    def pause():
        if tasks:
            tasks.pop(0)()

    scatter.start()
    out_line.start()
    for sequence in range(all_kept_ref.shape[0]):
        attend_back_sequence(
            q_heads,
            kv_heads,
            tile,
            pause,
            order_ref,
            where_ref,
            all_kept_ref.at[sequence],
            all_back_ref.at[sequence],
            all_lse_ref.at[sequence],
            cos_ref,
            sin_ref,
            all_out_ref.at[sequence],
            *work,
        )
    while tasks:
        pause()
    out_sum[...] = out_line.total().astype(jnp.bfloat16)
    out_line.finish()
    scatter.finish()


def attend_back_sequence(
    q_heads,
    kv_heads,
    tile,
    pause,
    order_ref,
    where_ref,
    kept_ref,
    back_ref,
    lse_ref,
    cos_ref,
    sin_ref,
    out_ref,
    back_sorted,
    grad,
    delta_ref,
    dq_ref,
):
    length, cols = kept_ref.shape
    blocks, rows = back_ref.shape[:2]
    group = q_heads // kv_heads
    q_cols, k_cols = q_heads * HEAD, kv_heads * HEAD
    scale = HEAD ** (-0.5)
    tiles = length // tile

    def take_block(i, _):
        start = pl.multiple_of(i * rows, rows)
        back_sorted[pl.ds(start, rows), :] = back_ref[where_ref[i]]
        return 0

    lax.fori_loop(0, blocks, take_block, 0)
    keep = causal_keep(tile)
    for kv in range(kv_heads):
        k_at = q_cols + kv * HEAD
        v_at = q_cols + k_cols + kv * HEAD

        def load(i, g):
            start = pl.multiple_of(i * tile, tile)
            head = kv * group + g
            at = slice(head * HEAD, (head + 1) * HEAD)
            return (
                kept_ref[pl.ds(start, tile), at],
                back_sorted[pl.ds(start, tile), at],
                lse_ref[head : head + 1, pl.ds(start, tile)],
            )

        def load_kv(j):
            start = pl.multiple_of(j * tile, tile)
            return (
                kept_ref[pl.ds(start, tile), k_at : k_at + HEAD],
                kept_ref[pl.ds(start, tile), v_at : v_at + HEAD],
            )

        def tile_terms(keys, values, query, back, lse, masked):
            weights = jnp.exp(dot_nt(keys, query) * scale - lse)
            if masked:
                weights = jnp.where(keep, weights, 0.0)
            return weights, dot_nt(values, back)

        def delta_step(i, _):
            rows_i = [load(i, g) for g in range(group)]

            def one(j, carry, masked):
                keys, values = load_kv(j)
                result = []
                for g in range(group):
                    weights, back_weights = tile_terms(keys, values, *rows_i[g], masked)
                    result.append(carry[g] + jnp.sum(weights * back_weights, 0, keepdims=True))
                return tuple(result)

            carry = tuple(jnp.zeros((1, tile), jnp.float32) for _ in range(group))
            carry = lax.fori_loop(0, i, lambda j, c: one(j, c, False), carry)
            carry = one(i, carry, True)
            for g in range(group):
                delta_ref[g : g + 1, pl.ds(pl.multiple_of(i * tile, tile), tile)] = carry[g]
            return 0

        lax.fori_loop(0, tiles, delta_step, 0)
        if kv == 0:
            pause()
        dq_ref[...] = jnp.zeros_like(dq_ref)

        def key_step(j, _):
            keys, values = load_kv(j)

            def one(i, carry, masked):
                back_key, back_value = carry
                start = pl.multiple_of(i * tile, tile)
                for g in range(group):
                    query, back, lse = load(i, g)
                    weights, back_weights = tile_terms(keys, values, query, back, lse, masked)
                    delta = delta_ref[g : g + 1, pl.ds(start, tile)]
                    back_scores = (weights * (back_weights - delta)).astype(jnp.bfloat16)
                    back_key = back_key + dot_nn(back_scores, query)
                    back_value = back_value + dot_nn(weights.astype(jnp.bfloat16), back)
                    dq_ref[g * HEAD : (g + 1) * HEAD, pl.ds(start, tile)] += dot_tn(
                        keys, back_scores
                    )
                return back_key, back_value

            zero = jnp.zeros((tile, HEAD), jnp.float32)
            carry = one(j, (zero, zero), True)
            carry = lax.fori_loop(j + 1, tiles, lambda i, c: one(i, c, False), carry)
            span = pl.ds(j * (tile // rows), tile // rows)
            grad[span, :, k_at : k_at + HEAD] = (carry[0] * scale).reshape(-1, rows, HEAD)
            grad[span, :, v_at : v_at + HEAD] = carry[1].reshape(-1, rows, HEAD)
            return 0

        lax.fori_loop(0, tiles, key_step, 0)
        for g in range(group):
            head = kv * group + g
            turned = (dq_ref[g * HEAD : (g + 1) * HEAD, :] * scale).T
            grad[:, :, head * HEAD : (head + 1) * HEAD] = turned.reshape(-1, rows, HEAD)

    def give_block(i, _):
        cos = cos_ref[order_ref[i]]
        sin = sin_ref[order_ref[i]]
        for c in range(0, cols, 2 * HEAD):
            values = grad[order_ref[i], :, c : c + 2 * HEAD]
            values = turn_columns(values, c, q_cols + k_cols, cos, sin, False)
            out_ref[i, :, c : c + 2 * HEAD] = values.astype(jnp.bfloat16)
        return 0

    lax.fori_loop(0, blocks, give_block, 0)


MESH = pl.DeviceIdType.MESH


def sequence_target(group, place, second, splits):
    sequence = 2 * group + second
    held_at = sequence % 4 * 2 + (sequence % 2 ^ sequence // 4)
    slot = place // 2
    target = (place % 2 * 2 + slot % 4 // 2, held_at * splits + slot // 4)
    return target, slot % 2


def token_target(group, place, half, splits):
    held_at = place // splits
    sequence = (held_at % 2 ^ held_at // 2 % 2) * 4 + held_at // 2
    slot = place % splits * 4 + group % 2 * 2 + half
    return (sequence // 2, 2 * slot + group // 2), sequence % 2


def remote(source, target, sems, device):
    return pltpu.make_async_remote_copy(
        src_ref=source,
        dst_ref=target,
        send_sem=sems[0],
        recv_sem=sems[1],
        device_id=device,
        device_id_type=MESH,
    )


def same(one, other):
    return jnp.logical_and(one[0] == other[0], one[1] == other[1])


def greet(me, peers, movers):
    barrier = pltpu.get_barrier_semaphore()
    for peer in peers:
        pl.semaphore_signal(barrier, inc=1, device_id=peer, device_id_type=MESH)
    expected = len(peers)
    for source, target in movers:

        @pl.when(jnp.logical_not(same(source, me)))
        def _():
            pl.semaphore_signal(barrier, inc=1, device_id=source, device_id_type=MESH)

        expected = expected + jnp.where(same(target, me), 0, 1)
    pl.semaphore_wait(barrier, expected)


def move_start(me, source, target, target_device, send, receive):
    here = same(target_device, me)

    @pl.when(here)
    def _():
        pltpu.make_async_copy(source, target, receive).start()

    @pl.when(jnp.logical_not(here))
    def _():
        remote(source, target, (send, receive), target_device).start()


def move_sent(me, source, target, target_device, send, receive):
    @pl.when(jnp.logical_not(same(target_device, me)))
    def _():
        remote(source, target, (send, receive), target_device).wait_send()


def member(me, by):
    return (me[0] ^ (by // 2), me[1] ^ (by % 2))


def group_index(device):
    return 2 * device[0] + device[1] % 2


class GroupExchange:
    def __init__(self, me, pieces, got, sems):
        self.me, self.pieces, self.got, self.sems = me, pieces, got, sems

    def hop(self, by):
        peer = member(self.me, by)
        sems = (self.sems.at[0, by - 1], self.sems.at[1, by - 1])
        return remote(
            self.pieces.at[group_index(peer)], self.got.at[group_index(self.me)], sems, peer
        )

    def own(self):
        mine = group_index(self.me)
        return pltpu.make_async_copy(self.pieces.at[mine], self.got.at[mine], self.sems.at[0, 7])

    def start(self):
        for by in range(1, 8):
            self.hop(by).start()
        self.own().start()

    def finish(self):
        self.own().wait()
        for by in range(1, 8):
            self.hop(by).wait()


class GroupGather:
    def __init__(self, me, rows, sems, own, window):
        self.rows, self.sems, self.own, self.window = rows, sems, own, window
        self.core, self.across, self.beside = member(me, 2), member(me, 4), member(me, 1)

    def hop(self, index):
        across, beside, core = self.across, self.beside, self.core
        source, i, j, half, device = (
            (None, 0, 2, 0, across),
            (None, 1, 0, 1, beside),
            (None, 1, 0, 0, beside),
            (None, 0, 2, 1, across),
            ((0, 2), 1, 2, 0, beside),
            ((1, 0), 1, 2, 1, across),
            (None, 0, 1, slice(0, 2), core),
            ((0, 2), 0, 3, slice(0, 2), core),
            ((1, 0), 1, 1, slice(0, 2), core),
            ((1, 2), 1, 3, slice(0, 2), core),
        )[index]
        if source is None:
            source = self.own.at[half, self.window]
        else:
            source = self.rows.at[source[0], source[1], half, self.window]
        target = self.rows.at[i, j, half, self.window]
        return remote(source, target, (self.sems.at[0, index], self.sems.at[1, index]), device)

    def start(self):
        for index in (0, 1, 2, 3, 6):
            self.hop(index).start()

    def pass_on(self):
        self.hop(0).wait_recv()
        self.hop(4).start()
        self.hop(1).wait_recv()
        self.hop(5).start()
        self.hop(3).wait_recv()
        self.hop(7).start()
        self.hop(2).wait_recv()
        self.hop(8).start()

    def finish(self):
        self.hop(4).wait_recv()
        self.hop(5).wait_recv()
        self.hop(9).start()
        for index in (6, 7, 8, 9):
            self.hop(index).wait_recv()
        for index in range(10):
            self.hop(index).wait_send()


class Moves:
    def __init__(self, me, splits, source, target, sems, back):
        self.me, self.splits, self.source, self.target = me, splits, source, target
        self.sems, self.back = sems, back

    def one(self, i):
        find = token_target if self.back else sequence_target
        device, place = find(self.me[0], self.me[1], i, self.splits)
        return (
            self.me,
            self.source.at[i],
            self.target.at[place],
            device,
            self.sems.at[0, i],
            self.sems.at[1, place],
        )

    def start(self):
        for i in (0, 1):
            move_start(*self.one(i))

    def wait_recv(self):
        for i in (0, 1):
            pltpu.make_async_copy(self.source.at[0], self.target.at[i], self.sems.at[1, i]).wait()

    def finish(self):
        for i in (0, 1):
            move_sent(*self.one(i))


def movers_of(me, splits, back):
    into = [sequence_target(me[0], me[1], i, splits)[0] for i in (0, 1)]
    home = [token_target(me[0], me[1], i, splits)[0] for i in (0, 1)]
    return list(zip(into, home)) if back else list(zip(home, into))


def first_kernel(shards, splits, tokens, pieces, out_own, gate_pieces, *refs):
    rows, in_all, out_all, gate_rows, held = refs[:5]
    move_sems, group_sems, piece_sems, gate_sems, own_sem, in_sems, out_sems = refs[5:]
    me = (lax.axis_index("dp"), lax.axis_index("ctx"))
    group, place = me
    slow = shards // 2
    slot = place // 2
    line = [(group, place ^ (2 * by)) for by in range(1, slow)]
    wanted, block = place // slow, place % slow
    takers = [(group, 2 * (slot ^ by) + wanted) for by in range(slow)]
    givers = [(group, place % 2 * slow + block_by) for block_by in range(slow)]
    movers = movers_of(me, splits, False) + list(zip(givers, takers))
    greet(me, [member(me, by) for by in range(1, 8)] + line, movers)
    swap = GroupExchange(me, pieces, held, piece_sems)
    gate_swap = GroupExchange(me, gate_pieces, gate_rows, gate_sems)
    move = Moves(me, splits, tokens, rows.at[0, 0], move_sems, False)

    def in_line(by):
        sems = (in_sems.at[0, by - 1], in_sems.at[1, by - 1])
        return remote(held, in_all.at[slot], sems, line[by - 1])

    def out_send(by):
        return (
            me,
            out_own,
            out_all.at[block],
            takers[by],
            out_sems.at[0, by],
            out_sems.at[1, block],
        )

    own = pltpu.make_async_copy(held, in_all.at[slot], own_sem)
    move.start()
    swap.start()
    gate_swap.start()
    swap.finish()
    move.wait_recv()
    spread = GroupGather(me, rows, group_sems, rows.at[0, 0], slice(0, tokens.shape[1]))
    spread.start()
    for by in range(1, slow):
        in_line(by).start()
    own.start()
    for by in range(slow):
        move_start(*out_send(by))
    spread.pass_on()
    for by in range(1, slow):
        in_line(by).wait()
    spread.finish()
    own.wait()
    for by in range(slow):
        pltpu.make_async_copy(out_own, out_all.at[by], out_sems.at[1, by]).wait()
    for by in range(slow):
        move_sent(*out_send(by))
    gate_swap.finish()
    move.finish()


def first_exchange(tokens, pieces, out_own, gate_pieces, shards, splits, identity):
    low = jnp.bfloat16
    slow = shards // 2
    any_space = pl.BlockSpec(memory_space=pl.ANY)
    dma = pltpu.SemaphoreType.DMA
    made = pl.pallas_call(
        functools.partial(first_kernel, shards, splits),
        out_shape=(
            jax.ShapeDtypeStruct((2, 4) + tokens.shape, low),
            jax.ShapeDtypeStruct((slow,) + pieces.shape, low),
            jax.ShapeDtypeStruct((slow,) + out_own.shape, low),
            jax.ShapeDtypeStruct(gate_pieces.shape, low),
            jax.ShapeDtypeStruct(pieces.shape, low),
        ),
        in_specs=[any_space] * 4,
        out_specs=(any_space,) * 5,
        scratch_shapes=[
            dma((2, 2)),
            dma((2, 10)),
            dma((2, 8)),
            dma((2, 8)),
            dma,
            dma((2, slow - 1)),
            dma((2, slow)),
        ],
        compiler_params=pltpu.CompilerParams(
            collective_id=identity, has_side_effects=True, vmem_limit_bytes=8 << 20
        ),
        cost_estimate=pl.CostEstimate(flops=0, bytes_accessed=200 << 20, transcendentals=0),
    )(tokens, pieces, out_own, gate_pieces)
    return made[:4]


class GroupScatter:
    def __init__(self, me, parts, buffers, sems, steps):
        self.parts = parts
        self.core_in, self.kept, self.sent, self.came, self.held = buffers[:5]
        self.sent_last, self.came_last = buffers[5:]
        self.core_sems, self.kept_sems, self.one_sems, self.last_sems = sems
        self.core, self.across, self.beside = member(me, 2), member(me, 4), member(me, 1)
        self.size = parts.shape[3] // steps
        self.steps = steps

    def window(self, k):
        return slice(k * self.size, (k + 1) * self.size)

    def to_core(self, k, j):
        return remote(
            self.parts.at[:, 2 * j + 1, :, self.window(k)],
            self.core_in.at[:, j, :, self.window(k)],
            (self.core_sems.at[0, k, j], self.core_sems.at[1, k, j]),
            self.core,
        )

    def keep(self, k, j):
        return pltpu.make_async_copy(
            self.parts.at[:, 2 * j, :, self.window(k)],
            self.kept.at[:, j, :, self.window(k)],
            self.kept_sems.at[k, j],
        )

    def first(self, k, half):
        return remote(
            self.sent.at[half, :, self.window(k)],
            self.came.at[half, :, self.window(k)],
            (self.one_sems.at[0, k, half], self.one_sems.at[1, k, half]),
            (self.beside, self.across)[half],
        )

    def second(self, k, half):
        return remote(
            self.sent_last.at[half, self.window(k)],
            self.came_last.at[half, self.window(k)],
            (self.last_sems.at[0, k, half], self.last_sems.at[1, k, half]),
            (self.across, self.beside)[half],
        )

    def start(self):
        for k in range(self.steps):
            for j in (0, 1):
                self.to_core(k, j).start()
                self.keep(k, j).start()

    def send_first(self, k):
        wide = jnp.float32
        rows = self.window(k)
        for j in (0, 1):
            self.keep(k, j).wait()
            self.to_core(k, j).wait_recv()
        for half in (0, 1):
            for other in (0, 1):
                at = (1, other) if half == 0 else (other, 1)
                both = self.kept[at[0], at[1], half, rows].astype(wide)
                both = both + self.core_in[at[0], at[1], half, rows].astype(wide)
                self.sent[half, other, rows] = both.astype(jnp.bfloat16)
            self.first(k, half).start()
        for half in (0, 1):
            for other in (0, 1):
                at = (0, other) if half == 0 else (other, 0)
                both = self.kept[at[0], at[1], half, rows].astype(wide)
                self.held[half, other, rows] = both + self.core_in[at[0], at[1], half, rows].astype(
                    wide
                )

    def send_second(self, k):
        wide = jnp.float32
        rows = self.window(k)
        for half in (0, 1):
            self.first(k, half).wait_recv()
            both = self.held[half, 1, rows] + self.came[half, 1, rows].astype(wide)
            self.sent_last[half, rows] = both.astype(jnp.bfloat16)
            self.second(k, half).start()
            self.held[half, 0, rows] = self.held[half, 0, rows] + self.came[half, 0, rows].astype(
                wide
            )

    def total(self, k, half):
        self.second(k, half).wait_recv()
        rows = self.window(k)
        return self.held[half, 0, rows] + self.came_last[half, rows].astype(jnp.float32)

    def finish(self):
        for k in range(self.steps):
            for j in (0, 1):
                self.to_core(k, j).wait_send()
            for half in (0, 1):
                self.first(k, half).wait_send()
                self.second(k, half).wait_send()


def scatter_scratch(rows, width, steps):
    low, wide = jnp.bfloat16, jnp.float32
    dma = pltpu.SemaphoreType.DMA
    return [
        pltpu.VMEM((2, 2, 2, rows, width), low),
        pltpu.VMEM((2, 2, 2, rows, width), low),
        pltpu.VMEM((2, 2, rows, width), low),
        pltpu.VMEM((2, 2, rows, width), low),
        pltpu.VMEM((2, 2, rows, width), wide),
        pltpu.VMEM((2, rows, width), low),
        pltpu.VMEM((2, rows, width), low),
        dma((2, steps, 2)),
        dma((steps, 2)),
        dma((2, steps, 2)),
        dma((2, steps, 2)),
    ]


def reordered(rows, slow, back):
    each = rows.shape[1] // (4 * slow)
    if back:
        starts = [s * 4 + dp for dp in range(4) for s in range(slow)]
    else:
        starts = [dp * slow + s for s in range(slow) for dp in range(4)]
    return jnp.concatenate([rows[:, i * each : (i + 1) * each] for i in starts], 1)


def turn_kernel(slow, steps, backward, parts, gain, *refs):
    if backward:
        residual, cot, result, gain_grad, rows = refs[:5]
        scratch = refs[5:]
    else:
        tokens, result, rows = refs[:3]
        scratch = refs[3:]
    own, own_sems, group_sems = scratch[:3]
    me = (lax.axis_index("dp"), lax.axis_index("ctx"))
    greet(me, [member(me, by) for by in (1, 2, 4)], [])
    scatter = GroupScatter(me, parts, scratch[3:10], scratch[10:], steps)
    gathers = [GroupGather(me, rows, group_sems.at[k], own, scatter.window(k)) for k in range(steps)]
    scatter.start()
    for k in range(steps):
        scatter.send_first(k)
    for k in range(steps):
        scatter.send_second(k)
    for k in range(steps):
        span = scatter.window(k)
        for half in (0, 1):
            total = scatter.total(k, half)
            if backward:
                values = residual[half, span]
                factor = lax.rsqrt(jnp.mean(values * values, -1, keepdims=True) + norm_eps)
                normed = values * factor
                total = reordered(total, slow, True)
                part = jnp.sum(total * normed, 0, keepdims=True)
                if k == 0 and half == 0:
                    gain_grad[...] = part
                else:
                    gain_grad[...] += part
                back = total * gain[...]
                back = factor * (back - normed * jnp.mean(back * normed, -1, keepdims=True))
                back = cot[half, span].astype(jnp.float32) + back
                result[half, span] = back
                own[half, span] = back.astype(jnp.bfloat16)
            else:
                values = tokens[half, span].astype(jnp.float32) + total
                factor = lax.rsqrt(jnp.mean(values * values, -1, keepdims=True) + norm_eps)
                result[half, span] = values
                own[half, span] = reordered(values * factor * gain[...], slow, False).astype(
                    jnp.bfloat16
                )
        gathers[k].start()
        keep = pltpu.make_async_copy(own.at[:, span], rows.at[0, 0, :, span], own_sems.at[k])
        keep.start()
    for k in range(steps):
        gathers[k].pass_on()
    for k in range(steps):
        gathers[k].finish()
        span = scatter.window(k)
        pltpu.make_async_copy(own.at[:, span], rows.at[0, 0, :, span], own_sems.at[k]).wait()
    scatter.finish()


def turn(parts, gain, rows_in, slow, backward, identity):
    low, wide = jnp.bfloat16, jnp.float32
    dma = pltpu.SemaphoreType.DMA
    rows, width = parts.shape[3:]
    steps = 2
    any_space = pl.BlockSpec(memory_space=pl.ANY)
    vmem = pl.BlockSpec(memory_space=pltpu.VMEM)
    shapes = [jax.ShapeDtypeStruct((2, rows, width), wide)]
    if backward:
        shapes.append(jax.ShapeDtypeStruct((1, width), wide))
    return pl.pallas_call(
        functools.partial(turn_kernel, slow, steps, backward),
        out_shape=tuple(shapes) + (jax.ShapeDtypeStruct((2, 4, 2, rows, width), low),),
        in_specs=[any_space, vmem] + [vmem] * len(rows_in),
        out_specs=tuple([vmem] * len(shapes) + [any_space]),
        scratch_shapes=[
            pltpu.VMEM((2, rows, width), low),
            dma((steps,)),
            dma((steps, 2, 10)),
        ]
        + scatter_scratch(rows, width, steps),
        compiler_params=pltpu.CompilerParams(
            collective_id=identity, has_side_effects=True, vmem_limit_bytes=48 << 20
        ),
        cost_estimate=pl.CostEstimate(flops=0, bytes_accessed=250 << 20, transcendentals=0),
    )(parts, gain, *rows_in)


def move_kernel(splits, tokens, rows, move_sems):
    me = (lax.axis_index("dp"), lax.axis_index("ctx"))
    greet(me, [], movers_of(me, splits, False))
    move = Moves(me, splits, tokens, rows, move_sems, False)
    move.start()
    move.wait_recv()
    move.finish()


def move_tokens(tokens, splits, identity):
    any_space = pl.BlockSpec(memory_space=pl.ANY)
    return pl.pallas_call(
        functools.partial(move_kernel, splits),
        out_shape=jax.ShapeDtypeStruct(tokens.shape, tokens.dtype),
        in_specs=[any_space],
        out_specs=any_space,
        scratch_shapes=[pltpu.SemaphoreType.DMA((2, 2))],
        compiler_params=pltpu.CompilerParams(
            collective_id=identity, has_side_effects=True, vmem_limit_bytes=4 << 20
        ),
        cost_estimate=pl.CostEstimate(flops=0, bytes_accessed=40 << 20, transcendentals=0),
    )(tokens)


def spread_kernel(own, rows, group_sems, own_sem):
    me = (lax.axis_index("dp"), lax.axis_index("ctx"))
    greet(me, [member(me, by) for by in (1, 2, 4)], [])
    gather = GroupGather(me, rows, group_sems, own, slice(0, own.shape[1]))
    keep = pltpu.make_async_copy(own, rows.at[0, 0], own_sem)
    gather.start()
    keep.start()
    gather.pass_on()
    gather.finish()
    keep.wait()


def spread_group(own, identity):
    any_space = pl.BlockSpec(memory_space=pl.ANY)
    dma = pltpu.SemaphoreType.DMA
    return pl.pallas_call(
        spread_kernel,
        out_shape=jax.ShapeDtypeStruct((2, 4) + own.shape, own.dtype),
        in_specs=[any_space],
        out_specs=any_space,
        scratch_shapes=[dma((2, 10)), dma],
        compiler_params=pltpu.CompilerParams(
            collective_id=identity, has_side_effects=True, vmem_limit_bytes=4 << 20
        ),
        cost_estimate=pl.CostEstimate(flops=0, bytes_accessed=100 << 20, transcendentals=0),
    )(own)


class LineSum:
    def __init__(self, me, slow, parts, buffers, sems):
        self.parts = parts
        self.kept, self.arrived = buffers
        self.sems, self.own_sem = sems
        self.slot = me[1] // 2
        self.slow = slow
        self.line = [(me[0], me[1] ^ (2 * by)) for by in range(1, slow)]

    def hop(self, by):
        sems = (self.sems.at[0, by - 1], self.sems.at[1, by - 1])
        return remote(
            self.parts.at[self.slot ^ by], self.arrived.at[by - 1], sems, self.line[by - 1]
        )

    def own(self):
        return pltpu.make_async_copy(self.parts.at[self.slot], self.kept, self.own_sem)

    def start(self):
        for by in range(1, self.slow):
            self.hop(by).start()
        self.own().start()

    def total(self):
        self.own().wait()
        value = self.kept[...].astype(jnp.float32)
        for by in range(1, self.slow):
            self.hop(by).wait_recv()
            value = value + self.arrived[by - 1].astype(jnp.float32)
        return value

    def finish(self):
        for by in range(1, self.slow):
            self.hop(by).wait_send()


def line_scratch(shape, kind, slow):
    dma = pltpu.SemaphoreType.DMA
    return [
        pltpu.VMEM(shape, kind),
        pltpu.VMEM((slow - 1,) + shape, kind),
        dma((2, slow - 1)),
        dma,
    ]


def last_kernel(shards, splits, steps, in_parts, out_done, gate_parts, in_back, made_two, *refs):
    gain, gain_two_grad, tokens, back_rows = refs[:4]
    in_total, out_total, gate_total, gains_total, tokens_grad, block_out = refs[4:10]
    scratch = list(refs[10:])

    def take(count):
        taken = scratch[:count]
        del scratch[:count]
        return taken

    me = (lax.axis_index("dp"), lax.axis_index("ctx"))
    group, place = me
    slow = shards // 2
    slot, half = place // 2, place % 2
    owned = in_parts.shape[2]
    home = (group, half * slow + slot)
    movers = movers_of(me, splits, True)
    movers.append(((group, place % slow * 2 + place // slow), home))
    line = [(group, place ^ (2 * by)) for by in range(1, slow)]
    greet(me, [member(me, by) for by in range(1, 8)] + line, movers)
    one = take(11)
    back_sum = GroupScatter(me, in_back, one[:7], one[7:], steps)
    line_in = take(4)
    line_gains = take(4)
    in_done, gains_own, gains_done, made_one, gain_grad = take(5)
    in_sems, gate_sems, gains_sems, one_sems, two_sems, home_sems = take(6)
    in_line = LineSum(me, slow, in_parts, line_in[:2], line_in[2:])
    gains_line = LineSum(me, slow, gains_own, line_gains[:2], line_gains[2:])
    in_swap = GroupExchange(me, in_done, in_total, in_sems)
    gate_swap = GroupExchange(me, gate_parts, gate_total, gate_sems)
    gains_swap = GroupExchange(me, gains_done, gains_total, gains_sems)
    move_grad = Moves(me, splits, made_one, tokens_grad, one_sems, True)
    move_out = Moves(me, splits, made_two, block_out, two_sems, True)
    back_sum.start()
    to_home = (me, out_done, out_total, home, home_sems.at[0], home_sems.at[1])
    in_line.start()
    move_start(*to_home)
    for k in range(steps):
        back_sum.send_first(k)
    move_out.start()
    for k in range(steps):
        back_sum.send_second(k)
    for k in range(steps):
        span = back_sum.window(k)
        for part in (0, 1):
            total = back_sum.total(k, part)
            values = tokens[part, span].astype(jnp.float32)
            normed, factor = norm_parts(values)
            grad = jnp.sum(total * normed, 0, keepdims=True)
            if k == 0 and part == 0:
                gain_grad[...] = grad
            else:
                gain_grad[...] += grad
            value = back_rows[part, span] + norm_back(total * gain[...], normed, factor)
            made_one[part, span] = value.astype(jnp.bfloat16)
    move_grad.start()
    gains_own[...] = jnp.zeros_like(gains_own)
    for dp in range(4):
        for s in range(slow):
            for side in range(2):
                at = ((dp * slow + s) * 2 + side) * owned
                index = 2 * dp + side
                gains_own[s, index, 0:1, 0:owned] = gain_grad[:, at : at + owned]
                gains_own[s, index, 0:1, owned : 2 * owned] = gain_two_grad[:, at : at + owned]
    gains_line.start()
    gate_swap.start()
    in_done[...] = in_line.total().astype(jnp.bfloat16)
    in_swap.start()
    gains_done[...] = gains_line.total()
    gains_swap.start()
    pltpu.make_async_copy(out_done, out_total, home_sems.at[1]).wait()
    move_sent(*to_home)
    for swap in (in_swap, gate_swap, gains_swap):
        swap.finish()
    for move in (move_out, move_grad):
        move.wait_recv()
        move.finish()
    for part in (in_line, gains_line, back_sum):
        part.finish()


def last_sums(
    in_parts, out_done, gate_parts, in_back, out_rows, others, shards, splits, identity
):
    low, wide = jnp.bfloat16, jnp.float32
    slow = shards // 2
    steps = 2
    any_space = pl.BlockSpec(memory_space=pl.ANY)
    vmem = pl.BlockSpec(memory_space=pltpu.VMEM)
    dma = pltpu.SemaphoreType.DMA
    rows, width = in_back.shape[3:]
    gains_shape = (8, 8, 128)
    moved = jax.ShapeDtypeStruct((2, rows, width), low)
    return pl.pallas_call(
        functools.partial(last_kernel, shards, splits, steps),
        out_shape=(
            jax.ShapeDtypeStruct(in_parts.shape[1:], low),
            jax.ShapeDtypeStruct(out_done.shape, low),
            jax.ShapeDtypeStruct(gate_parts.shape, low),
            jax.ShapeDtypeStruct(gains_shape, wide),
            moved,
            moved,
        ),
        in_specs=[any_space] * 5 + [vmem] * 4,
        out_specs=(any_space,) * 6,
        scratch_shapes=scatter_scratch(rows, width, steps)
        + line_scratch(in_parts.shape[1:], low, slow)
        + line_scratch(gains_shape, wide, slow)
        + [
            pltpu.VMEM(in_parts.shape[1:], low),
            pltpu.VMEM((slow,) + gains_shape, wide),
            pltpu.VMEM(gains_shape, wide),
            pltpu.VMEM(moved.shape, low),
            pltpu.VMEM((1, width), wide),
            dma((2, 8)),
            dma((2, 8)),
            dma((2, 8)),
            dma((2, 2)),
            dma((2, 2)),
            dma((2,)),
        ],
        compiler_params=pltpu.CompilerParams(
            collective_id=identity, has_side_effects=True, vmem_limit_bytes=56 << 20
        ),
        cost_estimate=pl.CostEstimate(flops=0, bytes_accessed=300 << 20, transcendentals=0),
    )(in_parts, out_done, gate_parts, in_back, out_rows, *others)


def position_tables(blocks, rows):
    frequency = rope_base ** (-(np.arange(HEAD // 2) * 2.0 / HEAD))
    angles = np.arange(blocks * rows).reshape(blocks, rows, 1) * frequency
    cos, sin = np.cos(angles), np.sin(angles)
    cosine = np.concatenate([cos, cos, cos, cos], 2)
    sines = np.concatenate([-sin, sin, -sin, sin], 2)
    return jnp.asarray(cosine, jnp.float32), jnp.asarray(sines, jnp.float32)


def attend(order, where, qkv, tables, q_heads, kv_heads):
    seqs, length, cols = qkv.shape
    blocks = order.shape[0]
    rows = length // blocks
    whole = pl.BlockSpec(memory_space=pltpu.VMEM)
    small = pl.BlockSpec(memory_space=pltpu.SMEM)
    return pl.pallas_call(
        functools.partial(attend_kernel, q_heads, kv_heads, 256),
        out_shape=(
            jax.ShapeDtypeStruct((seqs, blocks, rows, q_heads * HEAD), jnp.bfloat16),
            jax.ShapeDtypeStruct((seqs, q_heads, length), jnp.float32),
            jax.ShapeDtypeStruct((seqs, length, cols), jnp.bfloat16),
        ),
        in_specs=[small, small, whole, whole, whole],
        out_specs=(whole, whole, whole),
        scratch_shapes=[pltpu.VMEM((blocks, rows, q_heads * HEAD), jnp.bfloat16)],
        compiler_params=pltpu.CompilerParams(vmem_limit_bytes=40 << 20),
        cost_estimate=pl.CostEstimate(
            flops=2 * seqs * length * length * q_heads * HEAD,
            bytes_accessed=100 << 20,
            transcendentals=seqs * length * length * q_heads // 2,
        ),
    )(order, where, qkv.reshape(seqs, blocks, rows, cols), *tables)


def attend_back(
    order, where, kept, back, lse, tables, out_rows, residual, out_parts, q_heads, kv_heads, identity
):
    seqs, length, cols = kept.shape
    blocks = order.shape[0]
    block = length // blocks
    group = q_heads // kv_heads
    rows, width = out_rows.shape[3:]
    steps = 2
    whole = pl.BlockSpec(memory_space=pltpu.VMEM)
    small = pl.BlockSpec(memory_space=pltpu.SMEM)
    any_space = pl.BlockSpec(memory_space=pl.ANY)
    return pl.pallas_call(
        functools.partial(attend_back_kernel, q_heads, kv_heads, 256, steps),
        out_shape=(
            jax.ShapeDtypeStruct((seqs, blocks, block, cols), jnp.bfloat16),
            jax.ShapeDtypeStruct((2, rows, width), jnp.bfloat16),
            jax.ShapeDtypeStruct(out_parts.shape[1:], jnp.bfloat16),
        ),
        in_specs=[small, small] + [whole] * 5 + [any_space, whole, any_space],
        out_specs=(whole, whole, whole),
        scratch_shapes=[
            pltpu.VMEM((length, q_heads * HEAD), jnp.bfloat16),
            pltpu.VMEM((blocks, block, cols), jnp.float32),
            pltpu.VMEM((group, length), jnp.float32),
            pltpu.VMEM((group * HEAD, length), jnp.float32),
        ]
        + line_scratch(out_parts.shape[1:], jnp.bfloat16, out_parts.shape[0])
        + scatter_scratch(rows, width, steps),
        compiler_params=pltpu.CompilerParams(
            collective_id=identity, has_side_effects=True, vmem_limit_bytes=56 << 20
        ),
        cost_estimate=pl.CostEstimate(
            flops=7 * seqs * length * length * q_heads * HEAD,
            bytes_accessed=100 << 20,
            transcendentals=seqs * length * length * q_heads // 2,
        ),
    )(
        order,
        where,
        kept,
        back.reshape(seqs, blocks, block, -1),
        lse,
        *tables,
        out_rows,
        residual,
        out_parts,
    )


def gate_update_kernel(slow, step_rate, grad, weight, first, second, new_first, new_second, new):
    units = grad.shape[2] // slow
    pieces = [grad[half, :, s * units : (s + 1) * units] for s in range(slow) for half in (0, 1)]
    gradient = jnp.concatenate(pieces, 1).astype(jnp.float32)
    new_first[...], new_second[...], new[...] = adam_update(
        weight[...], gradient, first[...], second[...], step_rate, weight_decay
    )


def gate_update(grad, weight, first, second, slow, step_rate):
    rows, width = weight.shape
    block = pl.BlockSpec((rows, width // 8), lambda side, dp: (0, 4 * side + dp))
    piece = pl.BlockSpec((2, rows, width // 16), lambda side, dp: (dp, 0, side))
    return pl.pallas_call(
        functools.partial(gate_update_kernel, slow, step_rate),
        grid=(2, 4),
        out_shape=(jax.ShapeDtypeStruct(weight.shape, jnp.float32),) * 3,
        in_specs=[piece, block, block, block],
        out_specs=(block,) * 3,
        compiler_params=pltpu.CompilerParams(vmem_limit_bytes=32 << 20),
    )(grad, weight, first, second)


def local(
    tokens,
    cotangent,
    block_order,
    attention_in,
    attention_out,
    gate_up,
    down_matrix,
    gains,
    mean_attention_in,
    mean_attention_out,
    mean_gate_up,
    mean_down,
    mean_gains,
    square_attention_in,
    square_attention_out,
    square_gate_up,
    square_down,
    square_gains,
):
    seq_count, shard_rows, width = tokens.shape
    shards = lax.axis_size("ctx")
    slow = shards // 2
    mine = lax.axis_index("dp")
    beside = lax.axis_index("ctx") % 2
    low = jnp.bfloat16
    owned = attention_in.shape[0]
    hidden_units = gate_up.shape[1] // 2
    part_hidden = hidden_units // 8
    units = down_matrix.shape[0]
    part_q = HEADS * HEAD // 8
    part_k = KV_HEADS * HEAD // 8
    part_cols = part_q + 2 * part_k
    count = seq_count * shard_rows
    together = 8 * count
    spread = shards // (4 * seq_count)
    splits = max(1, slow // 8)
    seqs = 2 // spread if spread < 2 else 1
    length = shards * shard_rows
    q_heads = HEADS // 8 // splits
    kv_heads = KV_HEADS // 8

    in_low = attention_in.astype(low)
    gains_row = jnp.pad(gains.astype(low).reshape(1, -1), ((0, 15), (0, part_cols - 2 * owned)))
    pieces = jnp.stack(
        [
            jnp.concatenate(
                [
                    jnp.concatenate(
                        [
                            in_low[:, i * part_q : (i + 1) * part_q],
                            in_low[:, 8 * part_q + i * part_k :][:, :part_k],
                            in_low[:, 8 * (part_q + part_k) + i * part_k :][:, :part_k],
                        ],
                        1,
                    ),
                    gains_row,
                ]
            )
            for i in range(8)
        ]
    )
    gate_low = gate_up.astype(low)
    gate_pieces = jnp.stack(
        [
            jnp.concatenate(
                [
                    gate_low[:, side * hidden_units + (dp * shards + 2 * s + half) * units :][
                        :, :units
                    ]
                    for side in range(2)
                    for s in range(slow)
                ],
                1,
            )
            for dp in range(4)
            for half in range(2)
        ]
    )
    tokens_all, in_all, w_out, gate_rows = first_exchange(
        tokens, pieces, attention_out.astype(low), gate_pieces, shards, spread, 1
    )
    in_all = in_all.reshape(slow, 4, 2, owned + 16, part_cols).swapaxes(0, 1)
    w_in = in_all[:, :, :, :owned].reshape(width, part_cols)
    w_out = w_out.reshape(part_q, width)
    gains_all = in_all[:, :, :, owned, : 2 * owned].reshape(-1, 2, owned)
    gains_all = gains_all.astype(jnp.float32).swapaxes(0, 1).reshape(2, width)
    gain_one, gain_two = gains_all[0], gains_all[1]
    w_gate = gather_line(gate_rows.reshape(8 * owned, 2 * part_hidden))

    normed_all, _ = norm_parts(tokens_all.reshape(together, width).astype(jnp.float32))
    input_one = (normed_all * gain_one).astype(low)
    qkv = dot_nn(input_one, w_in)
    orders = block_order.reshape(spread, 2, 2, 2, -1).transpose(0, 3, 1, 2, 4)
    orders = orders.reshape(spread, 4, -1)
    slot_order = jnp.concatenate(
        [
            orders[(2 * s + (beside ^ i)) if spread > 1 else 0, mine ^ j]
            for s in range(splits)
            for i in range(2 // seqs)
            for j in range(4)
        ]
    )
    tables = position_tables(slot_order.shape[0], length // slot_order.shape[0])
    groups = [
        [2 * (s * splits + g) + half for g in range(splits)]
        for s in range(slow // splits)
        for half in (0, 1)
    ]

    def split_heads(values, widths, copies):
        parts = []
        start = 0
        for each, repeat in zip(widths, copies):
            kinds = splits // repeat
            piece = values[:, start : start + kinds * each].reshape(-1, kinds, each)
            parts.append(jnp.repeat(piece.swapaxes(0, 1), repeat, axis=0))
            start += kinds * each
        sent = jnp.concatenate(parts, 2)
        got = lax.all_to_all(sent, "ctx", 0, 0, axis_index_groups=groups, tiled=True)
        return got.reshape(length, -1)

    def join_heads(values):
        sent = values.reshape(splits, together, -1)
        return lax.all_to_all(sent, "ctx", 0, 0, axis_index_groups=groups, tiled=True)

    q_width, k_width = q_heads * HEAD, kv_heads * HEAD
    if splits > 1:
        qkv = split_heads(qkv, (q_width, k_width, k_width), (1, splits, splits))
    qkv = qkv.reshape(seqs, length, -1)
    blocks = slot_order.shape[0]
    slot_where = jnp.sum(
        jnp.where(
            slot_order[None, :] == jnp.arange(blocks, dtype=jnp.int32)[:, None],
            jnp.arange(blocks, dtype=jnp.int32)[None, :],
            0,
        ),
        1,
    )
    attended, lse, kept = attend(slot_order, slot_where, qkv, tables, q_heads, kv_heads)
    if splits > 1:
        attended = join_heads(attended.reshape(length, q_width)).swapaxes(0, 1)
    attended = attended.reshape(together, part_q)

    def parts(values):
        return values.astype(low).reshape((2, 4) + tokens.shape)

    residual_rows, input_two = turn(
        parts(dot_nn(attended, w_out)), gain_two[None], [tokens_all[0, 0]], slow, False, 3
    )
    input_two = input_two.reshape(together, width)
    after = 0.0 * (residual_rows[0, 0, 0] + w_gate[0, 0].astype(jnp.float32))
    cot_rows = move_tokens(cotangent + after.astype(low), spread, 7)
    after = 0.0 * cot_rows[0, 0, 0].astype(jnp.float32)
    w_down = gather_line((down_matrix + after).astype(low))
    gate_both = dot_nn(input_two, w_gate)
    gate_part = gate_both[:, :part_hidden]
    up_part = gate_both[:, part_hidden:]
    sigmoid_gate = jax.nn.sigmoid(gate_part)
    active = gate_part * sigmoid_gate
    hidden = lax.optimization_barrier((active * up_part).astype(low))
    back_all = spread_group(cot_rows + 0.0 * hidden[0, 0], 2).reshape(together, width)
    grad_down = lax.optimization_barrier(dot_tn(hidden, back_all).astype(low))
    down_sum = sum_line(grad_down + 0.0 * w_down[0, 0]).astype(jnp.float32)
    back_hidden = dot_nt(back_all, w_down + 0.0 * hidden[0, 0])
    back_gate = back_hidden * up_part * sigmoid_gate * (1.0 + gate_part * (1.0 - sigmoid_gate))
    back_upper = back_hidden * active
    back_gate_up = jnp.concatenate([back_gate, back_upper], 1).astype(low)
    gate_low = sum_line(dot_tn(input_two, back_gate_up).astype(low))
    back_rows, grad_gain_two, back_residual_all = turn(
        parts(dot_nt(back_gate_up, w_gate)),
        gain_two[None],
        [residual_rows, cot_rows],
        slow,
        True,
        4,
    )
    back_residual_all = back_residual_all.reshape(together, width)
    grad_out = dot_tn(attended, back_residual_all).astype(low)
    back_attended = dot_nt(back_residual_all, w_out).astype(low)
    if splits > 1:
        back_attended = split_heads(back_attended, (q_width,), (1,))
    back_projected, output_rows, out_sum = attend_back(
        slot_order,
        slot_where,
        kept,
        back_attended.reshape(seqs, length, -1),
        lse,
        tables,
        parts(dot_nn(hidden, w_down)),
        residual_rows,
        grad_out.reshape(slow, owned, width),
        q_heads,
        kv_heads,
        6,
    )
    if splits > 1:
        back_projected = join_heads(back_projected.reshape(length, -1)).astype(jnp.float32)
        back_projected = jnp.concatenate(
            [
                back_projected[..., :q_width].swapaxes(0, 1).reshape(together, part_q),
                back_projected[..., q_width:].sum(0),
            ],
            1,
        ).astype(low)
    back_projected = back_projected.reshape(together, part_cols)
    grad_in = dot_tn(input_one, back_projected).astype(low)
    grad_in = grad_in.reshape(4, slow, 2 * owned, part_cols).swapaxes(0, 1)
    in_sum, out_sum, gate_sum, gains_sum, tokens_grad, block_out = last_sums(
        grad_in.reshape(slow, 8, owned, part_cols),
        out_sum,
        gate_low.reshape(8, owned, 2 * part_hidden),
        parts(dot_nt(back_projected, w_in)),
        output_rows,
        [gain_one[None], grad_gain_two, tokens_all[0, 0], back_rows],
        shards,
        spread,
        5,
    )
    tokens_grad = tokens_grad.astype(jnp.float32)
    out_sum = out_sum.astype(jnp.float32)
    gains_sum = gains_sum[:, 0, : 2 * owned].reshape(8, 2, owned).sum(0)
    cuts = ((0, part_q), (part_q, part_q + part_k), (part_q + part_k, part_cols))
    in_sum = jnp.concatenate(
        [in_sum[i, :, first:last] for first, last in cuts for i in range(8)], 1
    ).astype(jnp.float32)
    new_in = adam_update(
        attention_in,
        in_sum,
        mean_attention_in,
        square_attention_in,
        input_boost * D ** (-0.5),
        weight_decay,
    )
    new_out = adam_update(
        attention_out,
        out_sum,
        mean_attention_out,
        square_attention_out,
        (HEADS * HEAD // 32) ** (-0.5),
        weight_decay,
    )
    new_gate = gate_update(
        gate_sum, gate_up, mean_gate_up, square_gate_up, slow, D ** (-0.5)
    )
    new_down = adam_update(
        down_matrix, down_sum, mean_down, square_down, FF ** (-0.5), weight_decay
    )
    new_gain = adam_update(gains, gains_sum, mean_gains, square_gains, gain_rate, 0.0)
    return (
        block_out,
        tokens_grad,
        new_in[0],
        new_in[1],
        new_in[2],
        new_out[0],
        new_out[1],
        new_out[2],
        new_gate[0],
        new_gate[1],
        new_gate[2],
        new_down[0],
        new_down[1],
        new_down[2],
        new_gain[0],
        new_gain[1],
        new_gain[2],
    )


def solution(mesh):
    in_specs = (
        P("dp", "ctx", None),
        P("dp", "ctx", None),
        P(),
        P(("dp", "ctx"), None),
        P(("dp", "ctx"), None),
        P(("dp", "ctx"), None),
        P(("dp", "ctx"), None),
        P(None, ("dp", "ctx")),
        P(("dp", "ctx"), None),
        P(("dp", "ctx"), None),
        P(("dp", "ctx"), None),
        P(("dp", "ctx"), None),
        P(None, ("dp", "ctx")),
        P(("dp", "ctx"), None),
        P(("dp", "ctx"), None),
        P(("dp", "ctx"), None),
        P(("dp", "ctx"), None),
        P(None, ("dp", "ctx")),
    )
    out_specs = (
        P("dp", "ctx", None),
        P("dp", "ctx", None),
        P(("dp", "ctx"), None),
        P(("dp", "ctx"), None),
        P(("dp", "ctx"), None),
        P(("dp", "ctx"), None),
        P(("dp", "ctx"), None),
        P(("dp", "ctx"), None),
        P(("dp", "ctx"), None),
        P(("dp", "ctx"), None),
        P(("dp", "ctx"), None),
        P(("dp", "ctx"), None),
        P(("dp", "ctx"), None),
        P(("dp", "ctx"), None),
        P(None, ("dp", "ctx")),
        P(None, ("dp", "ctx")),
        P(None, ("dp", "ctx")),
    )
    return jax.shard_map(local, mesh=mesh, in_specs=in_specs, out_specs=out_specs, check_vma=False)
```

profile of v0, /device:TPU:0, one launch (start us, length us, event | category | flops | bytes accessed | tf_op | source)
XLA Modules:
  0.0 807.6 jit_solution(12128322565995359994)
XLA Ops:
  21.6 101.9 %shard_map.323 = (bf16[2,4,2,128,2048]{4,3,2,1,0:T(8,128)(2,1)S(1)}, bf16[4,8,80,384]{3,2,1,0:T(8,128)(2,1)S(1)}, bf16[4,64,2048]{2,1,0:T(8,128)(2,1)S(1)}, bf16...) custom-call(bf16[2,128,2048]{2,1,0:T(8,128)(2,1)S(1)} %copy-done.13, ...), custom_call_target="tpu_custom_call" | custom-call | bytes 209715200 | tf_op jit(solution)/shard_map/pallas_call | solution.py:680
  134.5 5.1 fusion
  139.6 9.7 %fusion.2 = bf16[2,4,2,128,2048]{4,3,2,1,0:T(8,128)(2,1)} fusion(bf16[2,4,2,128,2048]{4,3,2,1,0:T(8,128)(2,1)} %copy-done, f32[2048]{0:T(1024)S(1)} %mul.220, f32[2,4,2,128]{3,2,1,0:T(2,128)S(1)} %add_rsqrt_fusion), kind=kLoop, calls=%fused_computation.4 | loop fusion | flops 16777216 | bytes 16793600 | tf_op jit(solution)/shard_map/convert_element_type | solution.py:1339
  149.4 7.0 fusion.46.all_qkv_ref
  156.4 32.7 %shard_map.324 = (bf16[2,16,64,256]{3,2,1,0:T(8,128)(2,1)S(1)}, f32[2,4,1024]{2,1,0:T(4,128)S(1)}, bf16[2,1024,384]{2,1,0:T(8,128)(2,1)S(1)}) custom-call(s32[16]{0:T(128)S(1)} %pad_add_fusion.order_ref, s32[16]{0:T(128)S(1)} %select_reduce_fusion.where_ref, f32[2,16,64,384]{3,2,1,0:T(8,128)S(1)} %fusion.46.all_qkv_ref, f32[16,64,128]{2,1,0:T(8,128)S(1)} %copy-done.17, ...), custom_call_target="tpu_custom_call" | custom-call | flops 1073741824 | bytes 104857600 | tf_op jit(solution)/shard_map/pallas_call | solution.py:1156
  189.2 5.6 convolution_convert_fusion.4
  196.2 81.5 %shard_map.325 = (f32[2,128,2048]{2,1,0:T(8,128)S(1)}, bf16[2,4,2,128,2048]{4,3,2,1,0:T(8,128)(2,1)}) custom-call(bf16[2,4,2,128,2048]{4,3,2,1,0:T(8,128)(2,1)} %bitcast.174, f32[1,2048]{1,0:T(1,128)S(1)} %slice.629.gain, bf16[2,128,2048]{2,1,0:T(8,128)(2,1)S(1)} %slice_bitcast_fusion.refs_0_.refs_2_), custom_call_target="tpu_custom_call" | custom-call | bytes 262144000 | tf_op jit(solution)/shard_map/pallas_call | solution.py:897
  287.0 20.5 %shard_map.326.refs_1_ = bf16[2,128,2048]{2,1,0:T(8,128)(2,1)S(1)} custom-call(bf16[2,128,2048]{2,1,0:T(8,128)(2,1)S(1)} %broadcast_add_fusion.2.tokens), custom_call_target="tpu_custom_call" | custom-call | bytes 41943040 | tf_op jit(solution)/shard_map/pallas_call | solution.py:926
  309.9 24.5 %fusion.47 = f32[2048,2048]{0,1:T(8,128)} fusion(bf16[2048,2048]{1,0:T(8,128)(2,1)} %bitcast.194, bf16[2048,2048]{1,0:T(8,128)(2,1)} %all-gather.3.cloned.1.call-done), kind=kOutput, calls=%fused_computation.191 | convolution fusion | flops 17179869184 | bytes 33554432 | tf_op jit(solution)/shard_map/dot_general | solution.py:71
  334.4 7.2 multiply_convert_fusion.2
  343.0 45.5 %shard_map.327 = bf16[2,4,2,128,2048]{4,3,2,1,0:T(8,128)(2,1)S(1)} custom-call(bf16[2,128,2048]{2,1,0:T(8,128)(2,1)S(1)} %broadcast_add_fusion.1.own), custom_call_target="tpu_custom_call" | custom-call | bytes 104857600 | tf_op jit(solution)/shard_map/pallas_call | solution.py:954
  391.8 10.4 %convolution_convert_fusion.5 = bf16[1024,2048]{1,0:T(8,128)(2,1)} fusion(bf16[2048,1024]{0,1:T(8,128)(2,1)S(1)} %multiply_convert_fusion.2, bf16[2048,2048]{1,0:T(8,128)(2,1)S(1)} %bitcast.169), kind=kOutput, calls=%fused_computation.18 | convolution fusion | flops 8592031744 | bytes 16777216 | tf_op jit(solution)/shard_map/dot_general | solution.py:79
  408.9 21.5 %multiply_convert_fusion.1 = (bf16[2048,1024]{0,1:T(8,128)(2,1)}, bf16[2048,1024]{0,1:T(8,128)(2,1)}) fusion(f32[2048,2048]{0,1:T(8,128)} %fusion.47, bf16[2048,2048]{1,0:T(8,128)(2,1)} %bitcast.170, bf16[1024,2048]{0,1:T(8,128)(2,1)} %all-gather.5.cloned.1.call-done, bf16[]{:T(256)} %bitcast.37), kind=kOutput, calls=%fused_computation.7 | convolution fusion | flops 8619294720 | bytes 37748736 | tf_op jit(solution)/shard_map/dot_general | solution.py:75
  430.4 23.7 %convolution_convert_fusion.1 = bf16[2048,2048]{1,0:T(8,128)(2,1)} fusion(bf16[2048,2048]{1,0:T(8,128)(2,1)} %bitcast.195, bf16[2048,1024]{0,1:T(8,128)(2,1)} %get-tuple-element.80, bf16[2048,1024]{0,1:T(8,128)(2,1)} %get-tuple-element.79), kind=kOutput, calls=%fused_computation.12 | convolution fusion | flops 17200840704 | bytes 25165824 | tf_op jit(solution)/shard_map/dot_general | solution.py:79
  455.5 24.3 %convolution_convert_fusion.3 = bf16[2048,2048]{1,0:T(8,128)(2,1)} fusion(bf16[2048,2048]{1,0:T(8,128)(2,1)} %all-gather.3.cloned.1.call-done, bf16[2048,1024]{0,1:T(8,128)(2,1)} %get-tuple-element.80, bf16[2048,1024]{0,1:T(8,128)(2,1)} %get-tuple-element.79), kind=kOutput, calls=%fused_computation.14 | convolution fusion | flops 17200840704 | bytes 25165824 | tf_op jit(solution)/shard_map/dot_general | solution.py:75
  479.9 78.4 %shard_map.328 = (f32[2,128,2048]{2,1,0:T(8,128)S(1)}, f32[1,2048]{1,0:T(1,128)S(1)}, bf16[2,4,2,128,2048]{4,3,2,1,0:T(8,128)(2,1)}) custom-call(bf16[2,4,2,128,2048]{4,3,2,1,0:T(8,128)(2,1)} %bitcast.180, f32[1,2048]{1,0:T(1,128)S(1)} %copy-done.19, f32[2,128,2048]{2,1,0:T(8,128)S(1)} %copy-done.7, bf16[2,128,2048]{2,1,0:T(8,128)(2,1)S(1)} %shard_map.326.refs_1_), custom_call_target="tpu_custom_call" | custom-call | bytes 262144000 | tf_op jit(solution)/shard_map/pallas_call | solution.py:897
  558.4 7.5 convolution_convert_fusion.7
  569.5 11.4 %convolution_convert_fusion.2 = bf16[2048,2048]{1,0:T(8,128)(2,1)} fusion(bf16[2048,1024]{0,1:T(8,128)(2,1)S(1)} %copy-done.29, bf16[1024,2048]{0,1:T(8,128)(2,1)S(1)} %copy-done.40), kind=kOutput, calls=%fused_computation.13 | convolution fusion | flops 8594128896 | bytes 16777216 | tf_op jit(solution)/shard_map/dot_general | solution.py:71
  580.9 57.9 %shard_map.329 = (bf16[2,16,64,384]{3,2,1,0:T(8,128)(2,1)}, bf16[2,128,2048]{2,1,0:T(8,128)(2,1)}, bf16[64,2048]{1,0:T(8,128)(2,1)}) custom-call(s32[16]{0:T(128)} %copy-done.22, s32[16]{0:T(128)} %copy-done.23, bf16[2,1024,384]{2,1,0:T(8,128)(2,1)} %copy-done.12, bf16[2,16,64,256]{3,2,1,0:T(8,128)(2,1)} %bitcast.190, f32[2,4,1024]{2,1,0:T(4,128)} %copy-done.20, ...), custom_call_target="tpu_custom_call" | custom-call | flops 3758096384 | bytes 104857600 | tf_op jit(solution)/shard_map/pallas_call | solution.py:1187
  638.8 8.5 %convolution_convert_fusion.6 = bf16[2048,384]{1,0:T(8,128)(2,1)S(1)} fusion(bf16[2048,2048]{1,0:T(8,128)(2,1)} %bitcast.178, bf16[2048,384]{1,0:T(8,128)(2,1)} %bitcast.196), kind=kOutput, calls=%fused_computation.20 | convolution fusion | flops 3222011904 | bytes 11534336 | tf_op jit(solution)/shard_map/dot_general | solution.py:79
  648.7 7.1 convolution_convert_fusion
  655.8 6.4 multiply_subtract_fusion
  662.2 110.6 %shard_map.330 = (bf16[8,64,384]{2,1,0:T(8,128)(2,1)}, bf16[64,2048]{1,0:T(8,128)(2,1)}, bf16[8,64,2048]{2,1,0:T(8,128)(2,1)}, f32[8,8,128]{2,1,0:T(8,128)}, bf1...) custom-call(bf16[4,8,64,384]{3,2,1,0:T(8,128)(2,1)} %bitcast.184, bf16[64,2048]{1,0:T(8,128)(2,1)} %get-tuple-element.52.out_done, ...), custom_call_target="tpu_custom_call" | custom-call | bytes 314572800 | tf_op jit(solution)/shard_map/pallas_call | solution.py:1106
  792.1 7.6 shard_map.331
  (166 shorter events, 72.5 us)
Async XLA Ops:
  7.2 276.0 %all-gather.3.cloned.1.call-start = ((), (), s32[]{:S(2)}) async-start(), calls=%async_computation.2 | async-start | bytes 10485760 | tf_op jit(solution)/shard_map/all_gather | solution.py:55
  20.8 106.1 %copy-start.39 = (s32[16]{0:T(128)S(1)}, s32[16]{0:T(128)}, u32[]{:S(2)}) copy-start(s32[16]{0:T(128)} %param.22) | copy-start | bytes 196
  126.8 62.4 %copy-start.14 = (bf16[4,64,2048]{2,1,0:T(8,128)(2,1)}, bf16[4,64,2048]{2,1,0:T(8,128)(2,1)S(1)}, u32[]{:S(2)}) copy-start(bf16[4,64,2048]{2,1,0:T(8,128)(2,1)S(1)} %get-tuple-element.45) | copy-start | bytes 3145732
  126.8 275.6 %all-gather.5.cloned.1.call-start = ((), (), s32[]{:S(2)}) async-start(), calls=%async_computation.3 | async-start | bytes 5242880 | tf_op jit(solution)/shard_map/all_gather | solution.py:55
  133.2 16.2 %copy-start.32 = (bf16[4,4,2,64,384]{4,3,2,1,0:T(8,128)(2,1)}, bf16[4,4,2,64,384]{4,3,2,1,0:T(8,128)(2,1)S(1)}, u32[]{:S(2)}) copy-start(bf16[4,4,2,64,384]{4,3,2,1,0:T(8,128)(2,1)S(1)} %copy.48) | copy-start | bytes 4718596
  134.2 61.9 %copy-start.18 = (f32[1,2048]{1,0:T(1,128)}, f32[1,2048]{1,0:T(1,128)S(1)}, u32[]{:S(2)}) copy-start(f32[1,2048]{1,0:T(1,128)S(1)} %slice.629.gain) | copy-start | bytes 24580
  134.4 22.0 %copy-start.22 = (s32[16]{0:T(128)}, s32[16]{0:T(128)S(1)}, u32[]{:S(2)}) copy-start(s32[16]{0:T(128)S(1)} %pad_add_fusion.order_ref) | copy-start | bytes 196
  134.5 21.9 %copy-start.23 = (s32[16]{0:T(128)}, s32[16]{0:T(128)S(1)}, u32[]{:S(2)}) copy-start(s32[16]{0:T(128)S(1)} %select_reduce_fusion.where_ref) | copy-start | bytes 196
  196.1 81.6 %copy-start.2 = (bf16[2,128,2048]{2,1,0:T(8,128)(2,1)}, bf16[2,128,2048]{2,1,0:T(8,128)(2,1)S(1)}, u32[]{:S(2)}) copy-start(bf16[2,128,2048]{2,1,0:T(8,128)(2,1)S(1)} %slice_bitcast_fusion.refs_0_.refs_2_) | copy-start | bytes 3145732
  277.7 31.0 %copy-start.26 = (f32[256,2048]{0,1:T(8,128)S(1)}, f32[256,2048]{0,1:T(8,128)}, u32[]{:S(2)}) copy-start(f32[256,2048]{0,1:T(8,128)} %copy.49) | copy-start | bytes 6291460
  309.9 345.9 %reduce-scatter.5.cloned.1.call-start = ((), (), s32[]{:S(2)}) async-start(), calls=%async_computation.5 | async-start | bytes 5242880 | tf_op jit(solution)/shard_map/reduce_scatter | solution.py:61
  341.6 46.9 %copy-start.28 = (bf16[2048,1024]{0,1:T(8,128)(2,1)}, bf16[2048,1024]{0,1:T(8,128)(2,1)S(1)}, u32[]{:S(2)}) copy-start(bf16[2048,1024]{0,1:T(8,128)(2,1)S(1)} %multiply_convert_fusion.2) | copy-start | bytes 12582916
  408.9 253.4 %reduce-scatter.3.cloned.1.call-start = ((), (), s32[]{:S(2)}) async-start(), calls=%async_computation.4 | async-start | bytes 10485760 | tf_op jit(solution)/shard_map/reduce_scatter | solution.py:61
  455.5 24.3 %copy-start.7 = (f32[2,128,2048]{2,1,0:T(8,128)S(1)}, f32[2,128,2048]{2,1,0:T(8,128)}, u32[]{:S(2)}) copy-start(f32[2,128,2048]{2,1,0:T(8,128)} %copy-done.6) | copy-start | bytes 6291460
  455.5 24.3 %copy-start.19 = (f32[1,2048]{1,0:T(1,128)S(1)}, f32[1,2048]{1,0:T(1,128)}, u32[]{:S(2)}) copy-start(f32[1,2048]{1,0:T(1,128)} %copy-done.18) | copy-start | bytes 24580
  479.9 78.5 %copy-start.4 = (bf16[2,16,64,256]{3,2,1,0:T(8,128)(2,1)S(1)}, bf16[2,16,64,256]{3,2,1,0:T(8,128)(2,1)}, u32[]{:S(2)}) copy-start(bf16[2,16,64,256]{3,2,1,0:T(8,128)(2,1)} %copy-done.3) | copy-start | bytes 3145732
  558.3 7.6 copy-start.11
  558.3 7.6 copy-start.21
  558.4 7.6 copy-start.15
  638.8 9.9 %copy-start.33 = (bf16[4,4,2,64,384]{4,3,2,1,0:T(8,128)(2,1)S(1)}, bf16[4,4,2,64,384]{4,3,2,1,0:T(8,128)(2,1)}, u32[]{:S(2)}) copy-start(bf16[4,4,2,64,384]{4,3,2,1,0:T(8,128)(2,1)} %copy-done.32) | copy-start | bytes 4718596
  638.8 9.9 %copy-start.41 = (bf16[2,16,64,384]{3,2,1,0:T(8,128)(2,1)S(1)}, bf16[2,16,64,384]{3,2,1,0:T(8,128)(2,1)}, u32[]{:S(2)}) copy-start(bf16[2,16,64,384]{3,2,1,0:T(8,128)(2,1)} %get-tuple-element.51) | copy-start | bytes 4718596
  772.9 7.6 copy-start.31
  772.9 11.5 %copy-start.30 = (f32[64,3072]{1,0:T(8,128)S(1)}, f32[64,3072]{1,0:T(8,128)}, u32[]{:S(2)}) copy-start(f32[64,3072]{1,0:T(8,128)} %param.23) | copy-start | bytes 2359300
  792.1 7.6 copy-start.34
  (22 other events, 105.1 us)
Sparse Core Ops, SparseCore 0:
  127.0 156.2 all-gather.2
  310.0 92.3 all-gather.4
  409.0 81.0 reduce-scatter.4
  492.4 161.6 reduce-scatter.2
where the time goes:
time: 821 us; the launch traced here: 808 us
  Pallas kernels  537 us (65%)
  matrix products  155 us (19%)
  other arithmetic  52 us (6%)
  local copies, waits for them, and re-layouts  41.4 us (5%)
  between operations  18.3 us (2%)
    pallas_call x2, Pallas kernels, turn(): pl.pallas_call(functools.partial(turn_kernel, slow, steps, backward), out...  160 us
    pallas_call x1, Pallas kernels, last_sums(): pl.pallas_call(functools.partial(last_kernel, shards, splits, steps), out...  111 us
    pallas_call x1, Pallas kernels, first_exchange(): pl.pallas_call(functools.partial(first_kernel, shards, splits), out_shape...  102 us
    pallas_call x1, Pallas kernels, attend_back(): pl.pallas_call(functools.partial(attend_back_kernel, q_heads, kv_heads, 2...  57.9 us
    dot_general x4, matrix products, dot_nt(): lax.dot_general(a, b, (((1,), (1,)), ((), ())), preferred_element_type=jn...  56.3 us
    dot_general x4, matrix products, dot_tn(): lax.dot_general(a, b, (((0,), (0,)), ((), ())), preferred_element_type=jn...  50.1 us
    dot_general x4, matrix products, dot_nn(): lax.dot_general(a, b, (((1,), (0,)), ((), ())), preferred_element_type=jn...  48.5 us
    pallas_call x1, Pallas kernels, spread_group(): pl.pallas_call(spread_kernel, out_shape=jax.ShapeDtypeStruct((2, 4) + own...  45.5 us
  transfers between devices with their start and end apart: 4, of which 2 were waited for; matrix products, arithmetic and copies ran while one was open for 24% of the time, Pallas kernels for 37%

commit v1 on v0

--- a/solution.py
+++ b/solution.py
@@ -1041,7 +1041,17 @@
     in_swap = GroupExchange(me, in_done, in_total, in_sems)
     gate_swap = GroupExchange(me, gate_parts, gate_total, gate_sems)
     gains_swap = GroupExchange(me, gains_done, gains_total, gains_sems)
-    move_grad = Moves(me, splits, made_one, tokens_grad, one_sems, True)
+    move_grads = [
+        Moves(
+            me,
+            splits,
+            made_one.at[:, back_sum.window(k)],
+            tokens_grad.at[:, back_sum.window(k)],
+            one_sems.at[k],
+            True,
+        )
+        for k in range(steps)
+    ]
     move_out = Moves(me, splits, made_two, block_out, two_sems, True)
     back_sum.start()
     to_home = (me, out_done, out_total, home, home_sems.at[0], home_sems.at[1])
@@ -1065,7 +1075,7 @@
                 gain_grad[...] += grad
             value = back_rows[part, span] + norm_back(total * gain[...], normed, factor)
             made_one[part, span] = value.astype(jnp.bfloat16)
-    move_grad.start()
+        move_grads[k].start()
     gains_own[...] = jnp.zeros_like(gains_own)
     for dp in range(4):
         for s in range(slow):
@@ -1084,7 +1094,7 @@
     move_sent(*to_home)
     for swap in (in_swap, gate_swap, gains_swap):
         swap.finish()
-    for move in (move_out, move_grad):
+    for move in [move_out] + move_grads:
         move.wait_recv()
         move.finish()
     for part in (in_line, gains_line, back_sum):
@@ -1127,7 +1137,7 @@
             dma((2, 8)),
             dma((2, 8)),
             dma((2, 8)),
-            dma((2, 2)),
+            dma((steps, 2, 2)),
             dma((2, 2)),
             dma((2,)),
         ],

time: 821 us -> 819 us (level)
  no operation moved by 1% of the time
where the time goes in v1:
time: 819 us; the launch traced here: 809 us
  Pallas kernels  538 us (66%)
  matrix products  155 us (19%)
  other arithmetic  52 us (6%)
  local copies, waits for them, and re-layouts  41.4 us (5%)
  between operations  18.3 us (2%)
    pallas_call x2, Pallas kernels, turn(): pl.pallas_call(functools.partial(turn_kernel, slow, steps, backward), out...  160 us
    pallas_call x1, Pallas kernels, last_sums(): pl.pallas_call(functools.partial(last_kernel, shards, splits, steps), out...  112 us
    pallas_call x1, Pallas kernels, first_exchange(): pl.pallas_call(functools.partial(first_kernel, shards, splits), out_shape...  102 us
    pallas_call x1, Pallas kernels, attend_back(): pl.pallas_call(functools.partial(attend_back_kernel, q_heads, kv_heads, 2...  57.9 us
    dot_general x4, matrix products, dot_nt(): lax.dot_general(a, b, (((1,), (1,)), ((), ())), preferred_element_type=jn...  56.3 us
    dot_general x4, matrix products, dot_tn(): lax.dot_general(a, b, (((0,), (0,)), ((), ())), preferred_element_type=jn...  50.1 us
    dot_general x4, matrix products, dot_nn(): lax.dot_general(a, b, (((1,), (0,)), ((), ())), preferred_element_type=jn...  48.5 us
    pallas_call x1, Pallas kernels, spread_group(): pl.pallas_call(spread_kernel, out_shape=jax.ShapeDtypeStruct((2, 4) + own...  45.5 us
  transfers between devices with their start and end apart: 4, of which 2 were waited for; matrix products, arithmetic and copies ran while one was open for 24% of the time, Pallas kernels for 37%

profile of v1, /device:TPU:0, one launch (start us, length us, event | category | flops | bytes accessed | tf_op | source)
XLA Modules:
  0.0 808.8 jit_solution(15957211651274928541)
XLA Ops:
  21.6 101.9 %shard_map.323 = (bf16[2,4,2,128,2048]{4,3,2,1,0:T(8,128)(2,1)S(1)}, bf16[4,8,80,384]{3,2,1,0:T(8,128)(2,1)S(1)}, bf16[4,64,2048]{2,1,0:T(8,128)(2,1)S(1)}, bf16...) custom-call(bf16[2,128,2048]{2,1,0:T(8,128)(2,1)S(1)} %copy-done.13, ...), custom_call_target="tpu_custom_call" | custom-call | bytes 209715200 | tf_op jit(solution)/shard_map/pallas_call | solution.py:680
  134.5 5.1 fusion
  139.6 9.7 %fusion.2 = bf16[2,4,2,128,2048]{4,3,2,1,0:T(8,128)(2,1)} fusion(bf16[2,4,2,128,2048]{4,3,2,1,0:T(8,128)(2,1)} %copy-done, f32[2048]{0:T(1024)S(1)} %mul.220, f32[2,4,2,128]{3,2,1,0:T(2,128)S(1)} %add_rsqrt_fusion), kind=kLoop, calls=%fused_computation.4 | loop fusion | flops 16777216 | bytes 16793600 | tf_op jit(solution)/shard_map/convert_element_type | solution.py:1349
  149.4 7.0 fusion.46.all_qkv_ref
  156.4 32.7 %shard_map.324 = (bf16[2,16,64,256]{3,2,1,0:T(8,128)(2,1)S(1)}, f32[2,4,1024]{2,1,0:T(4,128)S(1)}, bf16[2,1024,384]{2,1,0:T(8,128)(2,1)S(1)}) custom-call(s32[16]{0:T(128)S(1)} %pad_add_fusion.order_ref, s32[16]{0:T(128)S(1)} %select_reduce_fusion.where_ref, f32[2,16,64,384]{3,2,1,0:T(8,128)S(1)} %fusion.46.all_qkv_ref, f32[16,64,128]{2,1,0:T(8,128)S(1)} %copy-done.17, ...), custom_call_target="tpu_custom_call" | custom-call | flops 1073741824 | bytes 104857600 | tf_op jit(solution)/shard_map/pallas_call | solution.py:1166
  189.2 5.6 convolution_convert_fusion.4
  196.2 81.5 %shard_map.325 = (f32[2,128,2048]{2,1,0:T(8,128)S(1)}, bf16[2,4,2,128,2048]{4,3,2,1,0:T(8,128)(2,1)}) custom-call(bf16[2,4,2,128,2048]{4,3,2,1,0:T(8,128)(2,1)} %bitcast.174, f32[1,2048]{1,0:T(1,128)S(1)} %slice.629.gain, bf16[2,128,2048]{2,1,0:T(8,128)(2,1)S(1)} %slice_bitcast_fusion.refs_0_.refs_2_), custom_call_target="tpu_custom_call" | custom-call | bytes 262144000 | tf_op jit(solution)/shard_map/pallas_call | solution.py:897
  287.0 20.5 %shard_map.326.refs_1_ = bf16[2,128,2048]{2,1,0:T(8,128)(2,1)S(1)} custom-call(bf16[2,128,2048]{2,1,0:T(8,128)(2,1)S(1)} %broadcast_add_fusion.2.tokens), custom_call_target="tpu_custom_call" | custom-call | bytes 41943040 | tf_op jit(solution)/shard_map/pallas_call | solution.py:926
  309.9 24.5 %fusion.47 = f32[2048,2048]{0,1:T(8,128)} fusion(bf16[2048,2048]{1,0:T(8,128)(2,1)} %bitcast.194, bf16[2048,2048]{1,0:T(8,128)(2,1)} %all-gather.3.cloned.1.call-done), kind=kOutput, calls=%fused_computation.191 | convolution fusion | flops 17179869184 | bytes 33554432 | tf_op jit(solution)/shard_map/dot_general | solution.py:71
  334.4 7.2 multiply_convert_fusion.2
  343.0 45.5 %shard_map.327 = bf16[2,4,2,128,2048]{4,3,2,1,0:T(8,128)(2,1)S(1)} custom-call(bf16[2,128,2048]{2,1,0:T(8,128)(2,1)S(1)} %broadcast_add_fusion.1.own), custom_call_target="tpu_custom_call" | custom-call | bytes 104857600 | tf_op jit(solution)/shard_map/pallas_call | solution.py:954
  391.8 10.4 %convolution_convert_fusion.5 = bf16[1024,2048]{1,0:T(8,128)(2,1)} fusion(bf16[2048,1024]{0,1:T(8,128)(2,1)S(1)} %multiply_convert_fusion.2, bf16[2048,2048]{1,0:T(8,128)(2,1)S(1)} %bitcast.169), kind=kOutput, calls=%fused_computation.18 | convolution fusion | flops 8592031744 | bytes 16777216 | tf_op jit(solution)/shard_map/dot_general | solution.py:79
  408.9 21.5 %multiply_convert_fusion.1 = (bf16[2048,1024]{0,1:T(8,128)(2,1)}, bf16[2048,1024]{0,1:T(8,128)(2,1)}) fusion(f32[2048,2048]{0,1:T(8,128)} %fusion.47, bf16[2048,2048]{1,0:T(8,128)(2,1)} %bitcast.170, bf16[1024,2048]{0,1:T(8,128)(2,1)} %all-gather.5.cloned.1.call-done, bf16[]{:T(256)} %bitcast.37), kind=kOutput, calls=%fused_computation.7 | convolution fusion | flops 8619294720 | bytes 37748736 | tf_op jit(solution)/shard_map/dot_general | solution.py:75
  430.4 23.7 %convolution_convert_fusion.1 = bf16[2048,2048]{1,0:T(8,128)(2,1)} fusion(bf16[2048,2048]{1,0:T(8,128)(2,1)} %bitcast.195, bf16[2048,1024]{0,1:T(8,128)(2,1)} %get-tuple-element.80, bf16[2048,1024]{0,1:T(8,128)(2,1)} %get-tuple-element.79), kind=kOutput, calls=%fused_computation.12 | convolution fusion | flops 17200840704 | bytes 25165824 | tf_op jit(solution)/shard_map/dot_general | solution.py:79
  455.5 24.3 %convolution_convert_fusion.3 = bf16[2048,2048]{1,0:T(8,128)(2,1)} fusion(bf16[2048,2048]{1,0:T(8,128)(2,1)} %all-gather.3.cloned.1.call-done, bf16[2048,1024]{0,1:T(8,128)(2,1)} %get-tuple-element.80, bf16[2048,1024]{0,1:T(8,128)(2,1)} %get-tuple-element.79), kind=kOutput, calls=%fused_computation.14 | convolution fusion | flops 17200840704 | bytes 25165824 | tf_op jit(solution)/shard_map/dot_general | solution.py:75
  479.9 78.4 %shard_map.328 = (f32[2,128,2048]{2,1,0:T(8,128)S(1)}, f32[1,2048]{1,0:T(1,128)S(1)}, bf16[2,4,2,128,2048]{4,3,2,1,0:T(8,128)(2,1)}) custom-call(bf16[2,4,2,128,2048]{4,3,2,1,0:T(8,128)(2,1)} %bitcast.180, f32[1,2048]{1,0:T(1,128)S(1)} %copy-done.19, f32[2,128,2048]{2,1,0:T(8,128)S(1)} %copy-done.7, bf16[2,128,2048]{2,1,0:T(8,128)(2,1)S(1)} %shard_map.326.refs_1_), custom_call_target="tpu_custom_call" | custom-call | bytes 262144000 | tf_op jit(solution)/shard_map/pallas_call | solution.py:897
  558.4 7.5 convolution_convert_fusion.7
  569.5 11.4 %convolution_convert_fusion.2 = bf16[2048,2048]{1,0:T(8,128)(2,1)} fusion(bf16[2048,1024]{0,1:T(8,128)(2,1)S(1)} %copy-done.29, bf16[1024,2048]{0,1:T(8,128)(2,1)S(1)} %copy-done.40), kind=kOutput, calls=%fused_computation.13 | convolution fusion | flops 8594128896 | bytes 16777216 | tf_op jit(solution)/shard_map/dot_general | solution.py:71
  580.9 57.9 %shard_map.329 = (bf16[2,16,64,384]{3,2,1,0:T(8,128)(2,1)}, bf16[2,128,2048]{2,1,0:T(8,128)(2,1)}, bf16[64,2048]{1,0:T(8,128)(2,1)}) custom-call(s32[16]{0:T(128)} %copy-done.22, s32[16]{0:T(128)} %copy-done.23, bf16[2,1024,384]{2,1,0:T(8,128)(2,1)} %copy-done.12, bf16[2,16,64,256]{3,2,1,0:T(8,128)(2,1)} %bitcast.190, f32[2,4,1024]{2,1,0:T(4,128)} %copy-done.20, ...), custom_call_target="tpu_custom_call" | custom-call | flops 3758096384 | bytes 104857600 | tf_op jit(solution)/shard_map/pallas_call | solution.py:1197
  638.8 8.5 %convolution_convert_fusion.6 = bf16[2048,384]{1,0:T(8,128)(2,1)S(1)} fusion(bf16[2048,2048]{1,0:T(8,128)(2,1)} %bitcast.178, bf16[2048,384]{1,0:T(8,128)(2,1)} %bitcast.196), kind=kOutput, calls=%fused_computation.20 | convolution fusion | flops 3222011904 | bytes 11534336 | tf_op jit(solution)/shard_map/dot_general | solution.py:79
  648.7 7.1 convolution_convert_fusion
  655.8 6.4 multiply_subtract_fusion
  662.2 111.8 %shard_map.330 = (bf16[8,64,384]{2,1,0:T(8,128)(2,1)}, bf16[64,2048]{1,0:T(8,128)(2,1)}, bf16[8,64,2048]{2,1,0:T(8,128)(2,1)}, f32[8,8,128]{2,1,0:T(8,128)}, bf1...) custom-call(bf16[4,8,64,384]{3,2,1,0:T(8,128)(2,1)} %bitcast.184, bf16[64,2048]{1,0:T(8,128)(2,1)} %get-tuple-element.52.out_done, ...), custom_call_target="tpu_custom_call" | custom-call | bytes 314572800 | tf_op jit(solution)/shard_map/pallas_call | solution.py:1116
  793.3 7.6 shard_map.331
  (166 shorter events, 72.5 us)
Async XLA Ops:
  7.2 276.0 %all-gather.3.cloned.1.call-start = ((), (), s32[]{:S(2)}) async-start(), calls=%async_computation.2 | async-start | bytes 10485760 | tf_op jit(solution)/shard_map/all_gather | solution.py:55
  20.8 106.1 %copy-start.39 = (s32[16]{0:T(128)S(1)}, s32[16]{0:T(128)}, u32[]{:S(2)}) copy-start(s32[16]{0:T(128)} %param.22) | copy-start | bytes 196
  126.8 62.4 %copy-start.14 = (bf16[4,64,2048]{2,1,0:T(8,128)(2,1)}, bf16[4,64,2048]{2,1,0:T(8,128)(2,1)S(1)}, u32[]{:S(2)}) copy-start(bf16[4,64,2048]{2,1,0:T(8,128)(2,1)S(1)} %get-tuple-element.45) | copy-start | bytes 3145732
  126.8 275.6 %all-gather.5.cloned.1.call-start = ((), (), s32[]{:S(2)}) async-start(), calls=%async_computation.3 | async-start | bytes 5242880 | tf_op jit(solution)/shard_map/all_gather | solution.py:55
  133.2 16.2 %copy-start.32 = (bf16[4,4,2,64,384]{4,3,2,1,0:T(8,128)(2,1)}, bf16[4,4,2,64,384]{4,3,2,1,0:T(8,128)(2,1)S(1)}, u32[]{:S(2)}) copy-start(bf16[4,4,2,64,384]{4,3,2,1,0:T(8,128)(2,1)S(1)} %copy.48) | copy-start | bytes 4718596
  134.2 61.9 %copy-start.18 = (f32[1,2048]{1,0:T(1,128)}, f32[1,2048]{1,0:T(1,128)S(1)}, u32[]{:S(2)}) copy-start(f32[1,2048]{1,0:T(1,128)S(1)} %slice.629.gain) | copy-start | bytes 24580
  134.4 22.0 %copy-start.22 = (s32[16]{0:T(128)}, s32[16]{0:T(128)S(1)}, u32[]{:S(2)}) copy-start(s32[16]{0:T(128)S(1)} %pad_add_fusion.order_ref) | copy-start | bytes 196
  134.5 21.9 %copy-start.23 = (s32[16]{0:T(128)}, s32[16]{0:T(128)S(1)}, u32[]{:S(2)}) copy-start(s32[16]{0:T(128)S(1)} %select_reduce_fusion.where_ref) | copy-start | bytes 196
  196.1 81.6 %copy-start.2 = (bf16[2,128,2048]{2,1,0:T(8,128)(2,1)}, bf16[2,128,2048]{2,1,0:T(8,128)(2,1)S(1)}, u32[]{:S(2)}) copy-start(bf16[2,128,2048]{2,1,0:T(8,128)(2,1)S(1)} %slice_bitcast_fusion.refs_0_.refs_2_) | copy-start | bytes 3145732
  277.7 31.0 %copy-start.26 = (f32[256,2048]{0,1:T(8,128)S(1)}, f32[256,2048]{0,1:T(8,128)}, u32[]{:S(2)}) copy-start(f32[256,2048]{0,1:T(8,128)} %copy.49) | copy-start | bytes 6291460
  309.9 345.9 %reduce-scatter.5.cloned.1.call-start = ((), (), s32[]{:S(2)}) async-start(), calls=%async_computation.5 | async-start | bytes 5242880 | tf_op jit(solution)/shard_map/reduce_scatter | solution.py:61
  341.6 46.9 %copy-start.28 = (bf16[2048,1024]{0,1:T(8,128)(2,1)}, bf16[2048,1024]{0,1:T(8,128)(2,1)S(1)}, u32[]{:S(2)}) copy-start(bf16[2048,1024]{0,1:T(8,128)(2,1)S(1)} %multiply_convert_fusion.2) | copy-start | bytes 12582916
  408.9 253.4 %reduce-scatter.3.cloned.1.call-start = ((), (), s32[]{:S(2)}) async-start(), calls=%async_computation.4 | async-start | bytes 10485760 | tf_op jit(solution)/shard_map/reduce_scatter | solution.py:61
  455.5 24.3 %copy-start.7 = (f32[2,128,2048]{2,1,0:T(8,128)S(1)}, f32[2,128,2048]{2,1,0:T(8,128)}, u32[]{:S(2)}) copy-start(f32[2,128,2048]{2,1,0:T(8,128)} %copy-done.6) | copy-start | bytes 6291460
  455.5 24.3 %copy-start.19 = (f32[1,2048]{1,0:T(1,128)S(1)}, f32[1,2048]{1,0:T(1,128)}, u32[]{:S(2)}) copy-start(f32[1,2048]{1,0:T(1,128)} %copy-done.18) | copy-start | bytes 24580
  479.9 78.5 %copy-start.4 = (bf16[2,16,64,256]{3,2,1,0:T(8,128)(2,1)S(1)}, bf16[2,16,64,256]{3,2,1,0:T(8,128)(2,1)}, u32[]{:S(2)}) copy-start(bf16[2,16,64,256]{3,2,1,0:T(8,128)(2,1)} %copy-done.3) | copy-start | bytes 3145732
  558.3 7.6 copy-start.11
  558.3 7.6 copy-start.21
  558.4 7.6 copy-start.15
  638.8 9.9 %copy-start.33 = (bf16[4,4,2,64,384]{4,3,2,1,0:T(8,128)(2,1)S(1)}, bf16[4,4,2,64,384]{4,3,2,1,0:T(8,128)(2,1)}, u32[]{:S(2)}) copy-start(bf16[4,4,2,64,384]{4,3,2,1,0:T(8,128)(2,1)} %copy-done.32) | copy-start | bytes 4718596
  638.8 9.9 %copy-start.41 = (bf16[2,16,64,384]{3,2,1,0:T(8,128)(2,1)S(1)}, bf16[2,16,64,384]{3,2,1,0:T(8,128)(2,1)}, u32[]{:S(2)}) copy-start(bf16[2,16,64,384]{3,2,1,0:T(8,128)(2,1)} %get-tuple-element.51) | copy-start | bytes 4718596
  774.1 7.6 copy-start.31
  774.1 11.5 %copy-start.30 = (f32[64,3072]{1,0:T(8,128)S(1)}, f32[64,3072]{1,0:T(8,128)}, u32[]{:S(2)}) copy-start(f32[64,3072]{1,0:T(8,128)} %param.23) | copy-start | bytes 2359300
  793.3 7.6 copy-start.34
  (22 other events, 105.1 us)
Sparse Core Ops, SparseCore 0:
  127.0 156.2 all-gather.2
  310.0 92.3 all-gather.4
  409.0 81.0 reduce-scatter.4
  492.4 161.6 reduce-scatter.2
